TPU v7x, 128 devices: a whole 4x4x4 slice. The times are simulated.
128 devices in a mesh: fsdp: 32 (over z, x, core), feat: 4 (over y).
Axes of the slice: x: 4, y: 4, z: 4, core: 2. Of those that a mesh axis runs over, the one named last changes fastest.
Arguments:
- table_cells: bfloat16 [1536, 256, 192], P(('fsdp', 'feat'))
- attn_weights: bfloat16 [8, 192, 192], P(None, 'fsdp')
- hidden_up_weight: bfloat16 [192, 384], P('fsdp'), may hold values from -0.4375 to 0.4375
- hidden_down_weight: bfloat16 [384, 192], P('fsdp'), may hold values from -0.3125 to 0.3125
- norm_gains: float32 [3, 192], replicated, may hold values from 0.25 to 1.75
- train_count: int32 [1], replicated, may hold values from 384 to 1152
- feature_count: int32 [1], replicated, may hold values from 128 to 256
Outputs:
- layer_out: bfloat16 [1536, 256, 192], P(('fsdp', 'feat'))
Inputs may be any that keep to these rules, and one draw needn't show every extreme that they name: Rows 0 to train_count - 1 are the training rows. Features 0 to feature_count - 1 are real, the others padding.
All inputs are finite; a program needn't handle non-finite values.
Results may differ from a plain program's by a relative error of at most 0.012.
The roundings to bfloat16 on the way count: a program that leaves them out, or rounds other values in their place, can miss the bound.
Values may be sent and summed in bfloat16 or wider, within the bound.
A program may use at most 128 MiB of HBM per device.

v0:
```python
import jax
import jax.numpy as jnp
from jax import lax
from jax.sharding import PartitionSpec as P

HEADS = 6
EPS = 1e-05
NEGATIVE = -1e30


def normalize(value_rows, gain):
    floats = value_rows.astype(jnp.float32)
    average = jnp.mean(floats, axis=-1, keepdims=True)
    centered = floats - average
    variance = jnp.mean(centered * centered, axis=-1, keepdims=True)
    return (centered * lax.rsqrt(variance + EPS) * gain).astype(jnp.bfloat16)


def softmax_rows(scores, live):
    masked = jnp.where(live, scores, NEGATIVE)
    row_maximum = jnp.max(masked, axis=-1, keepdims=True)
    exponent = jnp.exp(masked - row_maximum)
    return (exponent / jnp.sum(exponent, axis=-1, keepdims=True)).astype(jnp.bfloat16)


def project(normed, weight):
    model_width = normed.shape[-1]
    product = jnp.dot(normed.reshape(-1, model_width), weight, preferred_element_type=jnp.float32)
    return product.astype(jnp.bfloat16).reshape(normed.shape[:-1] + (weight.shape[1],))


def output_proj(attended_rows, residual, weight):
    model_width = attended_rows.shape[-1]
    product = jnp.dot(
        attended_rows.reshape(-1, model_width), weight, preferred_element_type=jnp.float32
    )
    return (residual.astype(jnp.float32) + product.reshape(residual.shape)).astype(jnp.bfloat16)


def feature_attention(table_cells, normed, weights, feat_live):
    model_width = normed.shape[-1]
    head_size = model_width // HEADS
    queries = project(normed, weights[0])
    keys = project(normed, weights[1])
    value_rows = project(normed, weights[2])
    outputs = []
    for index_head in range(HEADS):
        training_extent = slice(index_head * head_size, (index_head + 1) * head_size)
        scores = jnp.einsum(
            "rqe,rke->rqk",
            queries[..., training_extent],
            keys[..., training_extent],
            preferred_element_type=jnp.float32,
        ) * head_size ** (-0.5)
        attention_probabilities = softmax_rows(scores, feat_live[None, None, :])
        outputs.append(
            jnp.einsum(
                "rqk,rke->rqe",
                attention_probabilities,
                value_rows[..., training_extent],
                preferred_element_type=jnp.float32,
            ).astype(jnp.bfloat16)
        )
    return output_proj(jnp.concatenate(outputs, axis=-1), table_cells, weights[3])


def sample_attention(column_block, normed, weights, row_live):
    all_rows, feat_here, model_width = normed.shape
    head_size = model_width // HEADS
    queries = project(normed, weights[4])
    keys = project(normed, weights[5])
    value_rows = project(normed, weights[6])
    block_count = max(1, all_rows // 512)
    block_rows = all_rows // block_count
    query_blocks = queries.reshape(block_count, block_rows, feat_here, model_width)

    def one_block(query_block):
        outputs = []
        for index_head in range(HEADS):
            training_extent = slice(index_head * head_size, (index_head + 1) * head_size)
            scores = jnp.einsum(
                "vsg,psg->svp",
                query_block[..., training_extent],
                keys[..., training_extent],
                preferred_element_type=jnp.float32,
            ) * head_size ** (-0.5)
            attention_probabilities = softmax_rows(scores, row_live[None, None, :])
            outputs.append(
                jnp.einsum(
                    "tdj,jtn->dtn",
                    attention_probabilities,
                    value_rows[..., training_extent],
                    preferred_element_type=jnp.float32,
                ).astype(jnp.bfloat16)
            )
        return jnp.concatenate(outputs, axis=-1)

    attended_rows = lax.map(one_block, query_blocks).reshape(all_rows, feat_here, model_width)
    return output_proj(attended_rows, column_block, weights[7])


def feed_forward(value_rows, gain, w_in, w_out):
    model_width = value_rows.shape[-1]
    normed = normalize(value_rows, gain)
    hidden = jnp.dot(normed.reshape(-1, model_width), w_in, preferred_element_type=jnp.float32)
    activated = jax.nn.gelu(hidden).astype(jnp.bfloat16)
    result = value_rows.astype(jnp.float32) + jnp.dot(
        activated, w_out, preferred_element_type=jnp.float32
    ).reshape(value_rows.shape)
    return result.astype(jnp.bfloat16)


def local(
    table_cells,
    attn_weights,
    hidden_up_weight,
    hidden_down_weight,
    norm_gains,
    train_count,
    feature_count,
):
    weights, w_in, w_out = (
        lax.all_gather(attn_weights, "fsdp", axis=1, tiled=True),
        lax.all_gather(hidden_up_weight, "fsdp", axis=0, tiled=True),
        lax.all_gather(hidden_down_weight, "fsdp", axis=0, tiled=True),
    )
    feat_live = jnp.arange(table_cells.shape[1]) < feature_count[0]
    normed_one = normalize(table_cells, norm_gains[0])
    mixed_rows = feature_attention(table_cells, normed_one, weights, feat_live)
    fsdp_size = lax.axis_size("fsdp")
    groups = lax.axis_size("feat")
    row_dev, feat_total, model_width = table_cells.shape
    devices_all = fsdp_size * groups
    all_rows = row_dev * devices_all
    train_limit = train_count[0]
    row_index = jnp.arange(all_rows)
    split_cells = mixed_rows.reshape(row_dev, devices_all, feat_total // devices_all, model_width)
    column_block = lax.all_to_all(
        split_cells, ("fsdp", "feat"), split_axis=1, concat_axis=0, tiled=True
    )
    rows_here, single, feat_here, width_here = column_block.shape
    owner_column_block = column_block.reshape(rows_here, feat_here, width_here)
    normed_two = normalize(owner_column_block, norm_gains[1])
    sampled = sample_attention(owner_column_block, normed_two, weights, row_index < train_limit)
    at_owners = sampled.reshape(rows_here, single, feat_here, width_here)
    returned = lax.all_to_all(at_owners, ("fsdp", "feat"), split_axis=0, concat_axis=1, tiled=True)
    returned = returned.reshape(row_dev, feat_total, model_width)
    returned = feed_forward(returned, norm_gains[2], w_in, w_out)
    return returned


def solution(mesh):
    in_specs = (
        P(("fsdp", "feat"), None, None),
        P(None, "fsdp", None),
        P("fsdp", None),
        P("fsdp", None),
        P(),
        P(),
        P(),
    )
    out_specs = P(("fsdp", "feat"), None, None)
    return jax.shard_map(local, mesh=mesh, in_specs=in_specs, out_specs=out_specs, check_vma=False)
```

profile of v0, /device:TPU:1, one launch (start us, length us, event | category | flops | bytes accessed | tf_op | source)
XLA Modules:
  0.0 370.8 jit_solution(5374347418670035218)
XLA Ops:
  0.0 27.7 %all_gather.9 = bf16[8,192,192]{2,0,1:T(8,128)(2,1)S(1)} all-gather(bf16[8,6,192]{2,0,1:T(8,128)(2,1)} %param.10), channel_id=1, replica_groups=mesh['fsdp'=32,'feat'=4] {'fsdp'}, dimensions={1}, use_global_device_ids=true | all-gather | bytes 608256 | tf_op jit(solution)/shard_map/all_gather | solution.py:123
  47.1 3.9 %fusion.417 = (f32[12,256]{1,0:T(8,128)S(1)}, f32[12,256,256]{1,2,0:T(8,128)}) fusion(pred[256]{0:T(512)(128)(4,1)S(1)} %iota_compare_fusion.1, bf16[12,256,32]{1,0,2:T(8,128)(2,1)} %get-tuple-element.136, bf16[12,256,32]{1,0,2:T(8,128)(2,1)} %get-tuple-element.106), kind=kOutput, calls=%fused_computation.353 | convolution fusion | flops 53477632 | bytes 3551488 | tf_op jit(solution)/shard_map/sub | solution.py:22
  51.0 4.0 %fusion.426 = (f32[12,256]{1,0:T(8,128)S(1)}, f32[12,256,256]{1,2,0:T(8,128)}) fusion(pred[256]{0:T(512)(128)(4,1)S(1)} %iota_compare_fusion.1, bf16[12,256,32]{1,0,2:T(8,128)(2,1)} %get-tuple-element.137, bf16[12,256,32]{1,0,2:T(8,128)(2,1)} %get-tuple-element.105), kind=kOutput, calls=%fused_computation.354 | convolution fusion | flops 53477632 | bytes 3551488 | tf_op jit(solution)/shard_map/sub | solution.py:22
  55.0 4.0 %fusion.435 = (f32[12,256]{1,0:T(8,128)S(1)}, f32[12,256,256]{1,2,0:T(8,128)}) fusion(pred[256]{0:T(512)(128)(4,1)S(1)} %iota_compare_fusion.1, bf16[12,256,32]{1,0,2:T(8,128)(2,1)} %get-tuple-element.138, bf16[12,256,32]{1,0,2:T(8,128)(2,1)} %get-tuple-element.104), kind=kOutput, calls=%fused_computation.355 | convolution fusion | flops 53477632 | bytes 3551488 | tf_op jit(solution)/shard_map/sub | solution.py:22
  84.9 7.2 %all-to-all-start = ((bf16[12,128,2,192]{3,2,0,1:T(2,128)(2,1)}), bf16[12,128,2,192]{3,2,0,1:T(2,128)(2,1)S(1)}, u32[]{:S(2)}, u32[]{:S(2)}) async-start(bf16[12,128,2,192]{3,2,0,1:T(2,128)(2,1)} %copy.182), calls=%async_computation | async-start | bytes 3145728 | tf_op jit(solution)/shard_map/all_to_all | solution.py:138
  92.9 24.1 %all-to-all-done = bf16[12,128,2,192]{3,2,0,1:T(2,128)(2,1)S(1)} async-done(((bf16[12,128,2,192]{3,2,0,1:T(2,128)(2,1)}), bf16[12,128,2,192]{3,2,0,1:T(2,128)(2,1)S(1)}, u32[]{:S(2)}, u32[]{:S(2)}) %all-to-all-start) | async-done | bytes 1179680 | tf_op jit(solution)/shard_map/all_to_all | solution.py:138
  118.9 4.0 %multiply_reduce_fusion.1 = f32[128,12,2]{2,1,0:T(8,128)S(1)} fusion(bf16[12,128,2,192]{3,2,0,1:T(2,128)(2,1)S(1)} %all-to-all-done, f32[128,12,2]{2,1,0:T(8,128)S(1)} %broadcast_multiply_fusion.1), kind=kLoop, calls=%fused_computation.190 | loop fusion | flops 2356224 | bytes 1204224 | tf_op jit(solution)/shard_map/reduce_sum | solution.py:15
  123.1 3.9 %multiply_convert_fusion.1 = bf16[128,12,1,2,192]{4,3,1,0,2:T(2,128)(2,1)S(1)} fusion(bf16[12,128,2,192]{3,2,0,1:T(2,128)(2,1)S(1)} %all-to-all-done, f32[192]{0:T(256)S(1)} %bitcast.148, f32[128,12,2]{2,1,0:T(8,128)S(1)} %add_rsqrt_fusion.1, f32[128,12,2]{2,1,0:T(8,128)S(1)} %broadcast_multiply_fusion.1), kind=kLoop, calls=%fused_computation.189 | loop fusion | flops 2949120 | bytes 2384640 | tf_op jit(solution)/shard_map/convert_element_type | solution.py:16
  134.0 4.9 %copy.190 = bf16[1536,2,192]{0,2,1:T(8,128)(2,1)} copy(bf16[1536,2,192]{2,1,0:T(2,128)(2,1)} %reshape.234) | data formatting | bytes 2359296
  144.4 4.9 %copy.191 = bf16[1536,2,192]{0,2,1:T(8,128)(2,1)} copy(bf16[1536,2,192]{2,1,0:T(2,128)(2,1)} %reshape.235) | data formatting | bytes 2359296
  152.6 105.7 %while.11 = (s32[]{:T(128)}, bf16[3,512,2,192]{1,3,2,0:T(8,128)(2,1)}, bf16[3,512,2,192]{1,3,2,0:T(8,128)(2,1)S(1)}, bf16[1536,2,192]{0,2,1:T(8,128)(2,1)}, bf16...) while((s32[]{:T(128)}, bf16[3,512,2,192]{1,3,2,0:T(8,128)(2,1)}, ...), condition=%wide.region_29.30_spmd.clone, body=%wide.region_16.29_spmd.clone.sunk | while | flops 1897096704 | bytes 11085937 | solution.py:98
  162.1 3.3 fusion.556
  167.5 3.3 fusion.558
  172.9 3.3 fusion.560
  197.1 3.3 fusion.556
  232.2 3.3 fusion.556
  262.0 3.3 copy.194
  270.7 3.9 %all-to-all-start.1 = ((bf16[1536,1,2,192]{3,2,1,0:T(2,128)(2,1)}), bf16[1536,1,2,192]{3,2,1,0:T(2,128)(2,1)S(1)}, u32[]{:S(2)}, u32[]{:S(2)}) async-start(bf16[1536,1,2,192]{3,2,1,0:T(2,128)(2,1)} %copy.195), calls=%async_computation.1 | async-start | bytes 3145728 | tf_op jit(solution)/shard_map/all_to_all | solution.py:146
  274.6 39.1 %all-gather.1 = bf16[32,12,192]{2,1,0:T(8,128)(2,1)S(1)} all-gather(bf16[1,12,192]{2,1,0:T(8,128)(2,1)S(1)} %bitcast.145), channel_id=1, replica_groups=mesh['fsdp'=32,'feat'=4] {'fsdp'}, dimensions={0}, use_global_device_ids=true | all-gather | bytes 152064 | tf_op jit(solution)/shard_map/all_gather | solution.py:125
  313.8 22.8 %all-gather = bf16[32,6,384]{2,1,0:T(8,128)(2,1)S(1)} all-gather(bf16[1,6,384]{2,1,0:T(8,128)(2,1)S(1)} %bitcast.146), channel_id=1, replica_groups=mesh['fsdp'=32,'feat'=4] {'fsdp'}, dimensions={0}, use_global_device_ids=true | all-gather | bytes 152064 | tf_op jit(solution)/shard_map/all_gather | solution.py:124
  339.6 5.1 %multiply_reduce_fusion = f32[12,128,2]{2,0,1:T(8,128)} fusion(bf16[128,12,1,2,192]{4,3,1,0,2:T(2,128)(2,1)S(1)} %bitcast.137, f32[12,128,2]{2,0,1:T(8,128)S(1)} %broadcast_multiply_fusion), kind=kLoop, calls=%fused_computation.188 | loop fusion | flops 2356224 | bytes 1204224 | tf_op jit(solution)/shard_map/reduce_sum | solution.py:15
  347.3 3.4 reshape.240
  350.8 3.4 reshape.239
  362.0 5.6 %fusion.235 = f32[3072,192]{0,1:T(8,128)} fusion(bf16[384,192]{1,0:T(8,128)(2,1)S(1)} %reshape.249, bf16[192,384]{1,0:T(8,128)(2,1)S(1)} %reshape.247, f32[3072,192]{1,0:T(8,128)} %reshape.240, f32[192]{0:T(256)S(1)} %bitcast.149, f32[3072]{0:T(1024)S(1)} %rsqrt.30, f32[3072]{0:T(1024)S(1)} %div.133), kind=kOutput, calls=%fused_computation.226 | convolution fusion | flops 918945792 | bytes 5038848 | tf_op jit(solution)/shard_map/dot_general | solution.py:107
  (159 shorter events, 177.1 us)
Async XLA Ops:
  0.0 29.8 %copy-start.18 = (f32[3,192]{1,0:T(4,128)S(1)}, f32[3,192]{1,0:T(4,128)}, u32[]{:S(2)}) copy-start(f32[3,192]{1,0:T(4,128)} %param.13) | copy-start | bytes 6916
  0.0 30.4 %copy-start.2 = (bf16[12,256,192]{1,2,0:T(8,128)(2,1)S(1)}, bf16[12,256,192]{1,2,0:T(8,128)(2,1)}, u32[]{:S(2)}) copy-start(bf16[12,256,192]{1,2,0:T(8,128)(2,1)} %param.9) | copy-start | bytes 3538948
  40.0 3.8 %copy-start.7 = (bf16[1,192,192]{2,0,1:T(2,128)(2,1)S(1)}, bf16[1,192,192]{2,0,1:T(2,128)(2,1)}, u32[]{:S(2)}) copy-start(bf16[1,192,192]{2,0,1:T(2,128)(2,1)} %get-tuple-element.118) | copy-start | bytes 221188
  64.7 2.9 copy-start.15
  67.6 2.4 copy-start.14
  67.6 2.9 copy-start.24
  72.6 2.0 copy-start.22
  82.6 9.4 %copy-start.6 = (bf16[1,192,192]{2,0,1:T(2,128)(2,1)S(1)}, bf16[1,192,192]{2,0,1:T(2,128)(2,1)}, u32[]{:S(2)}) copy-start(bf16[1,192,192]{2,0,1:T(2,128)(2,1)} %get-tuple-element.113) | copy-start | bytes 221188
  84.9 32.1 %all-to-all-start = ((bf16[12,128,2,192]{3,2,0,1:T(2,128)(2,1)}), bf16[12,128,2,192]{3,2,0,1:T(2,128)(2,1)S(1)}, u32[]{:S(2)}, u32[]{:S(2)}) async-start(bf16[12,128,2,192]{3,2,0,1:T(2,128)(2,1)} %copy.182), calls=%async_computation | async-start | bytes 3145728 | tf_op jit(solution)/shard_map/all_to_all | solution.py:138
  117.0 6.0 %copy-start = (bf16[12,128,2,192]{3,2,0,1:T(2,128)(2,1)}, bf16[12,128,2,192]{3,2,0,1:T(2,128)(2,1)S(1)}, u32[]{:S(2)}) copy-start(bf16[12,128,2,192]{3,2,0,1:T(2,128)(2,1)S(1)} %all-to-all-done) | copy-start | bytes 3538948
  123.1 5.4 %copy-start.10 = (bf16[1,192,192]{2,0,1:T(2,128)(2,1)S(1)}, bf16[1,192,192]{2,0,1:T(2,128)(2,1)}, u32[]{:S(2)}) copy-start(bf16[1,192,192]{2,0,1:T(2,128)(2,1)} %get-tuple-element.120) | copy-start | bytes 221188
  131.9 7.1 %copy-start.9 = (bf16[1,192,192]{2,0,1:T(2,128)(2,1)S(1)}, bf16[1,192,192]{2,0,1:T(2,128)(2,1)}, u32[]{:S(2)}) copy-start(bf16[1,192,192]{2,0,1:T(2,128)(2,1)} %get-tuple-element.119) | copy-start | bytes 221188
  142.3 7.0 %copy-start.8 = (bf16[1,192,192]{2,0,1:T(2,128)(2,1)S(1)}, bf16[1,192,192]{2,0,1:T(2,128)(2,1)}, u32[]{:S(2)}) copy-start(bf16[1,192,192]{2,0,1:T(2,128)(2,1)} %get-tuple-element.114) | copy-start | bytes 221188
  153.5 3.1 copy-start.5
  188.6 3.1 copy-start.5
  223.6 3.1 copy-start.5
  258.4 2.5 copy-start.1
  261.9 3.4 copy-start.11
  267.8 6.8 %copy-start.16 = (bf16[12,192]{1,0:T(8,128)(2,1)S(1)}, bf16[12,192]{1,0:T(8,128)(2,1)}, u32[]{:S(2)}) copy-start(bf16[12,192]{1,0:T(8,128)(2,1)} %param.12) | copy-start | bytes 13828
  267.8 46.0 %copy-start.17 = (bf16[6,384]{1,0:T(8,128)(2,1)S(1)}, bf16[6,384]{1,0:T(8,128)(2,1)}, u32[]{:S(2)}) copy-start(bf16[6,384]{1,0:T(8,128)(2,1)} %param.11) | copy-start | bytes 13828
  270.7 66.0 %all-to-all-start.1 = ((bf16[1536,1,2,192]{3,2,1,0:T(2,128)(2,1)}), bf16[1536,1,2,192]{3,2,1,0:T(2,128)(2,1)S(1)}, u32[]{:S(2)}, u32[]{:S(2)}) async-start(bf16[1536,1,2,192]{3,2,1,0:T(2,128)(2,1)} %copy.195), calls=%async_computation.1 | async-start | bytes 3145728 | tf_op jit(solution)/shard_map/all_to_all | solution.py:146
  354.2 5.6 %copy-start.3 = (f32[12,256,192]{2,1,0:T(8,128)S(1)}, f32[12,256,192]{2,1,0:T(8,128)}, u32[]{:S(2)}) copy-start(f32[12,256,192]{2,1,0:T(8,128)} %reshape.239) | copy-start | bytes 7077892
  358.3 3.7 copy-start.19
  362.0 5.6 %copy-start.4 = (f32[12,256,192]{1,2,0:T(8,128)S(1)}, f32[12,256,192]{1,2,0:T(8,128)}, u32[]{:S(2)}) copy-start(f32[12,256,192]{1,2,0:T(8,128)} %copy.203) | copy-start | bytes 7077892
  (5 other events, 7.7 us)
where the time goes:
time: 378 us; the launch traced here: 371 us
  matrix products  143 us (38%)
  blocking collectives  89.6 us (24%)
  local copies, waits for them, and re-layouts  74.2 us (20%)
  other arithmetic  26.4 us (7%)
  waiting for transfers between devices  24.1 us (6%)
  starting transfers between devices  11 us (3%)
    sub x24, matrix products, softmax_rows(): exponent = jnp.exp(masked - row_maximum)  62.1 us
    dot_general x18, matrix products, one_block(): jnp.einsum('tdj,jtn->dtn', attention_probabilities, value_rows[..., train...  59.2 us
    all_gather x1, blocking collectives, local(): lax.all_gather(hidden_down_weight, 'fsdp', axis=0, tiled=True)  39.1 us
    all_gather x1, blocking collectives, local(): lax.all_gather(attn_weights, 'fsdp', axis=1, tiled=True)  27.7 us
    all_to_all x1, waiting for transfers between devices, local(): lax.all_to_all(split_cells, ('fsdp', 'feat'), split_axis=1, concat_axis=0...  24.1 us
    all_gather x1, blocking collectives, local(): lax.all_gather(hidden_up_weight, 'fsdp', axis=0, tiled=True)  22.8 us
    unnamed x55, local copies, waits for them, and re-layouts  18.9 us
    reshape x5, local copies, waits for them, and re-layouts, project(): product.astype(jnp.bfloat16).reshape(normed.shape[:-1] + (weight.shape[1],))  10.6 us
  transfers between devices with their start and end apart: 2, of which 1 were waited for; matrix products, arithmetic and copies ran while one was open for 0% of the time, Pallas kernels for 0%

commit v1 on v0

--- a/solution.py
+++ b/solution.py
@@ -135,8 +135,14 @@
     train_limit = train_count[0]
     row_index = jnp.arange(all_rows)
     split_cells = mixed_rows.reshape(row_dev, devices_all, feat_total // devices_all, model_width)
-    column_block = lax.all_to_all(
-        split_cells, ("fsdp", "feat"), split_axis=1, concat_axis=0, tiled=True
+    column_block = jnp.concatenate(
+        lax.all_to_all(
+            jnp.stack(jnp.split(split_cells, lax.axis_size(("fsdp", "feat")), axis=1)),
+            ("fsdp", "feat"),
+            0,
+            0,
+        ),
+        axis=0,
     )
     rows_here, single, feat_here, width_here = column_block.shape
     owner_column_block = column_block.reshape(rows_here, feat_here, width_here)

time: 378 us -> 468 us (1.24)
  local copies, waits for them, and re-layouts: 74.2 us -> 150 us
  loops' own time: 0.67 us -> 17.7 us
    unnamed x55 -> x182, local copies, waits for them, and re-layouts: 18.9 us -> 96.4 us
    another operation x1, loops' own time: 0.67 us -> 17.7 us  [sample_attention(): lax.map(one_block, query_blocks).reshape(all_rows, feat_here, model_width)]
where the time goes in v1:
time: 468 us; the launch traced here: 462 us
  local copies, waits for them, and re-layouts  150 us (32%)
  matrix products  143 us (31%)
  blocking collectives  89.5 us (19%)
  other arithmetic  25.1 us (5%)
  waiting for transfers between devices  24.1 us (5%)
  loops' own time  17.7 us (4%)
  starting transfers between devices  11.2 us (2%)
    unnamed x182, local copies, waits for them, and re-layouts  96.4 us
    sub x24, matrix products, softmax_rows(): exponent = jnp.exp(masked - row_maximum)  62.1 us
    dot_general x18, matrix products, one_block(): jnp.einsum('tdj,jtn->dtn', attention_probabilities, value_rows[..., train...  59.2 us
    all_gather x1, blocking collectives, local(): lax.all_gather(hidden_down_weight, 'fsdp', axis=0, tiled=True)  39.2 us
    all_gather x1, blocking collectives, local(): lax.all_gather(attn_weights, 'fsdp', axis=1, tiled=True)  27.5 us
    all_to_all x1, waiting for transfers between devices, local(): lax.all_to_all(jnp.stack(jnp.split(split_cells, lax.axis_size(('fsdp', 'f...  24.1 us
    all_gather x1, blocking collectives, local(): lax.all_gather(hidden_up_weight, 'fsdp', axis=0, tiled=True)  22.8 us
    another operation x1, loops' own time, sample_attention(): lax.map(one_block, query_blocks).reshape(all_rows, feat_here, model_width)  17.7 us
  transfers between devices with their start and end apart: 2, of which 1 were waited for; matrix products, arithmetic and copies ran while one was open for 0% of the time, Pallas kernels for 0%

profile of v1, /device:TPU:1, one launch (start us, length us, event | category | flops | bytes accessed | tf_op | source)
XLA Modules:
  0.0 461.6 jit_solution(2638384497584270838)
XLA Ops:
  0.0 27.5 %all_gather.9 = bf16[8,192,192]{2,0,1:T(8,128)(2,1)S(1)} all-gather(bf16[8,6,192]{2,0,1:T(8,128)(2,1)} %param.10), channel_id=1, replica_groups=mesh['fsdp'=32,'feat'=4] {'fsdp'}, dimensions={1}, use_global_device_ids=true | all-gather | bytes 608256 | tf_op jit(solution)/shard_map/all_gather | solution.py:123
  46.9 3.9 fusion.417
  50.9 4.0 fusion.426
  54.8 4.0 fusion.435
  160.8 7.2 %all-to-all-start = ((bf16[128,12,1,2,192]{4,3,1,2,0:T(2,128)(2,1)}), bf16[128,12,1,2,192]{4,3,1,2,0:T(2,128)(2,1)S(1)}, u32[]{:S(2)}, u32[]{:S(2)}) async-start(bf16[128,12,1,2,192]{4,3,1,2,0:T(2,128)(2,1)} %constant_dynamic-update-slice_fusion), calls=%async_computation | async-start | bytes 3145728 | tf_op jit(solution)/shard_map/all_to_all | solution.py:139
  168.8 24.1 %all-to-all-done = bf16[128,12,1,2,192]{4,3,1,2,0:T(2,128)(2,1)S(1)} async-done(((bf16[128,12,1,2,192]{4,3,1,2,0:T(2,128)(2,1)}), bf16[128,12,1,2,192]{4,3,1,2,0:T(2,128)(2,1)S(1)}, u32[]{:S(2)}, u32[]{:S(2)}) %all-to-all-start) | async-done | bytes 1179680 | tf_op jit(solution)/shard_map/all_to_all | solution.py:139
  194.8 4.0 multiply_reduce_fusion.1
  199.0 3.9 multiply_convert_fusion.1
  210.0 4.9 %copy.816 = bf16[1536,2,192]{0,2,1:T(8,128)(2,1)} copy(bf16[1536,2,192]{2,1,0:T(2,128)(2,1)} %reshape.228) | data formatting | bytes 2359296
  220.4 4.9 %copy.817 = bf16[1536,2,192]{0,2,1:T(8,128)(2,1)} copy(bf16[1536,2,192]{2,1,0:T(2,128)(2,1)} %reshape.229) | data formatting | bytes 2359296
  228.6 122.8 %while.11 = (s32[]{:T(128)}, bf16[3,512,2,192]{1,3,2,0:T(8,128)(2,1)}, bf16[3,512,2,192]{1,3,2,0:T(8,128)(2,1)S(1)}, bf16[1536,2,192]{0,2,1:T(8,128)(2,1)}, bf16...) while((s32[]{:T(128)}, bf16[3,512,2,192]{1,3,2,0:T(8,128)(2,1)}, ...), condition=%wide.region_29.30_spmd.clone, body=%wide.region_16.29_spmd.clone.sunk | while | flops 1897096704 | bytes 11085937 | solution.py:98
  249.8 3.3 fusion.554
  255.2 3.3 fusion.556
  260.6 3.3 fusion.558
  284.8 3.3 fusion.554
  290.2 3.3 fusion.556
  295.7 3.3 fusion.558
  361.4 4.0 all-to-all-start.1
  365.4 39.2 %all-gather.1 = bf16[32,12,192]{2,1,0:T(8,128)(2,1)S(1)} all-gather(bf16[1,12,192]{2,1,0:T(8,128)(2,1)S(1)} %bitcast.896), channel_id=1, replica_groups=mesh['fsdp'=32,'feat'=4] {'fsdp'}, dimensions={0}, use_global_device_ids=true | all-gather | bytes 152064 | tf_op jit(solution)/shard_map/all_gather | solution.py:125
  404.7 22.8 %all-gather = bf16[32,6,384]{2,1,0:T(8,128)(2,1)S(1)} all-gather(bf16[1,6,384]{2,1,0:T(8,128)(2,1)S(1)} %bitcast.897), channel_id=1, replica_groups=mesh['fsdp'=32,'feat'=4] {'fsdp'}, dimensions={0}, use_global_device_ids=true | all-gather | bytes 152064 | tf_op jit(solution)/shard_map/all_gather | solution.py:124
  430.4 5.1 %multiply_reduce_fusion = f32[12,128,2]{2,0,1:T(8,128)} fusion(bf16[128,12,1,2,192]{4,3,1,0,2:T(2,128)(2,1)S(1)} %bitcast.889, f32[12,128,2]{2,0,1:T(8,128)S(1)} %broadcast_multiply_fusion), kind=kLoop, calls=%fused_computation.186 | loop fusion | flops 2356224 | bytes 1204224 | tf_op jit(solution)/shard_map/reduce_sum | solution.py:15
  438.2 3.4 reshape.234
  441.6 3.4 reshape.233
  452.8 5.6 %fusion.235 = f32[3072,192]{0,1:T(8,128)} fusion(bf16[384,192]{1,0:T(8,128)(2,1)S(1)} %reshape.241, bf16[192,384]{1,0:T(8,128)(2,1)S(1)} %reshape.239, f32[3072,192]{1,0:T(8,128)} %reshape.234, f32[192]{0:T(256)S(1)} %bitcast.900, f32[3072]{0:T(1024)S(1)} %rsqrt.30, f32[3072]{0:T(1024)S(1)} %div.133), kind=kOutput, calls=%fused_computation.225 | convolution fusion | flops 918945792 | bytes 5038848 | tf_op jit(solution)/shard_map/dot_general | solution.py:107
  (285 shorter events, 250.7 us)
Async XLA Ops:
  27.5 2.2 copy-start.18
  27.5 2.7 copy-start.2
  64.6 2.9 copy-start.15
  67.5 2.4 copy-start.14
  67.5 2.9 copy-start.24
  70.4 2.0 copy-start.23
  72.4 2.0 copy-start.22
  74.4 1.9 copy-start.21
  76.3 1.9 copy-start.20
  160.8 7.2 %copy-start.6 = (bf16[1,192,192]{2,0,1:T(2,128)(2,1)S(1)}, bf16[1,192,192]{2,0,1:T(2,128)(2,1)}, u32[]{:S(2)}) copy-start(bf16[1,192,192]{2,0,1:T(2,128)(2,1)} %get-tuple-element.113) | copy-start | bytes 221188
  160.8 32.1 %all-to-all-start = ((bf16[128,12,1,2,192]{4,3,1,2,0:T(2,128)(2,1)}), bf16[128,12,1,2,192]{4,3,1,2,0:T(2,128)(2,1)S(1)}, u32[]{:S(2)}, u32[]{:S(2)}) async-start(bf16[128,12,1,2,192]{4,3,1,2,0:T(2,128)(2,1)} %constant_dynamic-update-slice_fusion), calls=%async_computation | async-start | bytes 3145728 | tf_op jit(solution)/shard_map/all_to_all | solution.py:139
  193.0 6.0 %copy-start = (bf16[128,12,1,2,192]{4,3,1,2,0:T(2,128)(2,1)}, bf16[128,12,1,2,192]{4,3,1,2,0:T(2,128)(2,1)S(1)}, u32[]{:S(2)}) copy-start(bf16[128,12,1,2,192]{4,3,1,2,0:T(2,128)(2,1)S(1)} %all-to-all-done) | copy-start | bytes 3538948
  210.0 4.9 %copy-start.9 = (bf16[1,192,192]{2,0,1:T(2,128)(2,1)S(1)}, bf16[1,192,192]{2,0,1:T(2,128)(2,1)}, u32[]{:S(2)}) copy-start(bf16[1,192,192]{2,0,1:T(2,128)(2,1)} %get-tuple-element.119) | copy-start | bytes 221188
  220.4 4.9 %copy-start.8 = (bf16[1,192,192]{2,0,1:T(2,128)(2,1)S(1)}, bf16[1,192,192]{2,0,1:T(2,128)(2,1)}, u32[]{:S(2)}) copy-start(bf16[1,192,192]{2,0,1:T(2,128)(2,1)} %get-tuple-element.114) | copy-start | bytes 221188
  246.6 3.1 copy-start.5
  281.7 3.1 copy-start.5
  316.7 3.1 copy-start.5
  353.2 3.2 copy-start.11
  361.4 4.0 copy-start.16
  361.4 43.3 %copy-start.17 = (bf16[6,384]{1,0:T(8,128)(2,1)S(1)}, bf16[6,384]{1,0:T(8,128)(2,1)}, u32[]{:S(2)}) copy-start(bf16[6,384]{1,0:T(8,128)(2,1)} %param.11) | copy-start | bytes 13828
  361.4 66.1 %all-to-all-start.1 = ((bf16[1536,1,2,192]{3,2,1,0:T(2,128)(2,1)}), bf16[1536,1,2,192]{3,2,1,0:T(2,128)(2,1)S(1)}, u32[]{:S(2)}, u32[]{:S(2)}) async-start(bf16[1536,1,2,192]{3,2,1,0:T(2,128)(2,1)} %copy.821), calls=%async_computation.1 | async-start | bytes 3145728 | tf_op jit(solution)/shard_map/all_to_all | solution.py:152
  446.4 4.2 copy-start.3
  450.6 2.2 copy-start.19
  452.8 5.6 %copy-start.4 = (f32[12,256,192]{1,2,0:T(8,128)S(1)}, f32[12,256,192]{1,2,0:T(8,128)}, u32[]{:S(2)}) copy-start(f32[12,256,192]{1,2,0:T(8,128)} %copy.829) | copy-start | bytes 7077892
  (5 other events, 6.3 us)
